TPU v7x, 32 devices: a whole 2x2x4 slice. The times are simulated.
32 devices in a mesh: groups: 1, expert: 8 (over z, y), fsdp: 2 (over x), dp: 2 (over core).
Axes of the slice: x: 2, y: 2, z: 4, core: 2. Of those that a mesh axis runs over, the one named last changes fastest.
Arguments:
- moe_input: bfloat16 [4096, 1024], P(('groups', 'expert', 'fsdp', 'dp')), may hold values from -6 to 6
- moe_gain: float32 [1024], replicated, may hold values from 0.2 to 2
- routes: int32 [4096, 10], P(('groups', 'expert', 'fsdp', 'dp')), may hold values from 0 to 31, all different within a row; in each aligned block of 128 rows (0 to 127, 128 to 255, ...) at most 50 rows name the same one
- route_gates: float32 [4096, 10], P(('groups', 'expert', 'fsdp', 'dp')), may hold values from 0.05 to 0.2
- expert_gate: bfloat16 [32, 1024, 512], P(('expert', 'dp'), None, 'fsdp'), may hold values from -0.1875 to 0.1875
- expert_up: bfloat16 [32, 1024, 512], P(('expert', 'dp'), None, 'fsdp'), may hold values from -0.1875 to 0.1875
- expert_down: bfloat16 [32, 512, 1024], P(('expert', 'dp'), 'fsdp'), may hold values from -0.25 to 0.25
- shared_gate: bfloat16 [1024, 512], P(None, 'fsdp'), may hold values from -0.1875 to 0.1875
- shared_up: bfloat16 [1024, 512], P(None, 'fsdp'), may hold values from -0.1875 to 0.1875
- shared_down: bfloat16 [512, 1024], P('fsdp'), may hold values from -0.25 to 0.25
- shared_switch: float32 [1024], replicated, may hold values from -0.5 to 0.5
- mixed_qkv: bfloat16 [32, 128, 4096], P(('groups', 'expert', 'fsdp', 'dp')), may hold values from -6 to 6
- out_gate: bfloat16 [32, 128, 2048], P(('groups', 'expert', 'fsdp', 'dp')), may hold values from -6 to 6
- beta_logit: float32 [32, 128, 16], P(('groups', 'expert', 'fsdp', 'dp')), may hold values from -6 to 6
- step_logit: float32 [32, 128, 16], P(('groups', 'expert', 'fsdp', 'dp')), may hold values from -6 to 6
- conv_weight: float32 [4, 4096], replicated, may hold values from -3 to 3
- decay_log: float32 [16], replicated, may hold values from -3 to 1.5
- decay_bias: float32 [16], replicated, may hold values from -2 to 2
- head_gain: float32 [128], replicated, may hold values from 0.2 to 2
- lengths: int32 [32], P(('groups', 'expert', 'fsdp', 'dp')), may hold values from 32 to 128, as said below
Outputs:
- moe_output: bfloat16 [4096, 1024], P(('groups', 'expert', 'fsdp', 'dp'))
- core_output: bfloat16 [32, 128, 2048], P(('groups', 'expert', 'fsdp', 'dp'))
Inputs may be any that keep to these rules, and one draw needn't show every extreme that they name: `routes`: the rows of one device name each expert at most 50 times, a bound that some block reaches. `lengths`: some request is live at all 128 positions.
All inputs are finite; a program needn't handle non-finite values.
Results may differ from a plain program's by a relative error of at most 0.0069.
Values may be sent and summed in bfloat16 or wider, within the bound.
A program may use at most 128 MiB of HBM per device.

v0:
```python
import math

import jax
import jax.numpy as jnp
from jax import lax
from jax.sharding import PartitionSpec as P

EPS = 1e-06
HIGHEST = lax.Precision.HIGHEST


def normalize_rows(rows, gain):
    widened = rows.astype(jnp.float32)
    factor = lax.rsqrt(jnp.mean(widened * widened, axis=-1, keepdims=True) + EPS)
    return widened * factor * gain


def expert_rows(rows, w_gate, w_up, w_down):
    gate_part = jnp.dot(rows, w_gate, preferred_element_type=jnp.float32)
    up_part = jnp.dot(rows, w_up, preferred_element_type=jnp.float32)
    hidden = (jax.nn.silu(gate_part) * up_part).astype(jnp.bfloat16)
    return jnp.dot(hidden, w_down, preferred_element_type=jnp.float32)


def conv_silu(streams, conv_weight):
    widened = streams.astype(jnp.float32)
    kernel_size = conv_weight.shape[0]
    length = widened.shape[1]
    padded = jnp.pad(widened, ((0, 0), (kernel_size - 1, 0), (0, 0)))
    summed = jnp.zeros_like(widened)
    for offset in range(kernel_size):
        summed = summed + conv_weight[offset] * padded[:, offset : offset + length]
    return jax.nn.silu(summed)


def unit_vectors(vectors):
    return vectors * lax.rsqrt(jnp.sum(vectors * vectors, axis=-1, keepdims=True) + EPS)


def prepare_heads(mixed_qkv, beta_logit, step_logit, conv_weight, decay_log, decay_bias, head_gain):
    streams = conv_silu(mixed_qkv, conv_weight)
    batch_count, length, channels = streams.shape
    head_size = head_gain.shape[0]
    value_heads = decay_log.shape[0]
    key_heads = (channels - value_heads * head_size) // (2 * head_size)
    key_span = key_heads * head_size
    queries = unit_vectors(
        streams[:, :, :key_span].reshape(batch_count, length, key_heads, head_size)
    )
    queries = queries * (1.0 / math.sqrt(head_size))
    keys_all = unit_vectors(
        streams[:, :, key_span : 2 * key_span].reshape(batch_count, length, key_heads, head_size)
    )
    values = streams[:, :, 2 * key_span :].reshape(batch_count, length, value_heads, head_size)
    repeat = value_heads // key_heads
    queries = jnp.repeat(queries, repeat, axis=2)
    keys_all = jnp.repeat(keys_all, repeat, axis=2)
    beta_gate = jax.nn.sigmoid(beta_logit)
    decays = -jnp.exp(decay_log) * jax.nn.softplus(step_logit + decay_bias)
    return (queries, keys_all, values, beta_gate, decays)


def gated_output(attended, out_gate, head_gain, lengths):
    batch_count, length, heads_count, head_size = attended.shape
    normed = normalize_rows(attended, head_gain)
    gate_now = out_gate.astype(jnp.float32).reshape(batch_count, length, heads_count, head_size)
    gated_rows = (normed * jax.nn.silu(gate_now)).reshape(
        batch_count, length, heads_count * head_size
    )
    positions = jnp.arange(length, dtype=jnp.int32)
    live_mask = positions[None, :] < lengths[:, None]
    return jnp.where(live_mask[:, :, None], gated_rows, 0.0).astype(jnp.bfloat16)


def block_rule(memory, pieces):
    queries, keys_all, values, beta_gate, decays = pieces
    block_size = decays.shape[-1]
    running = jnp.cumsum(decays, axis=-1)
    lower_mask = jnp.tril(jnp.ones((block_size, block_size), dtype=bool))
    strict_mask = jnp.tril(jnp.ones((block_size, block_size), dtype=bool), -1)
    spread = running[..., :, None] - running[..., None, :]
    factors = jnp.where(lower_mask, jnp.exp(jnp.where(lower_mask, spread, 0.0)), 0.0)
    growth = jnp.exp(running)
    key_key = jnp.einsum("nhid,nhjd->nhij", keys_all, keys_all, precision=HIGHEST)
    system = jnp.where(strict_mask, beta_gate[..., :, None] * key_key * factors, 0.0) + jnp.eye(
        block_size, dtype=jnp.float32
    )
    recalled = jnp.einsum("nhid,nhde->nhie", keys_all, memory, precision=HIGHEST)
    target = beta_gate[..., None] * (values - growth[..., None] * recalled)
    update = jax.scipy.linalg.solve_triangular(system, target, lower=True, unit_diagonal=True)
    scores = jnp.einsum("nhid,nhjd->nhij", queries, keys_all, precision=HIGHEST) * factors
    result = growth[..., None] * jnp.einsum("nhid,nhde->nhie", queries, memory, precision=HIGHEST)
    result = result + jnp.einsum("nhij,nhje->nhie", scores, update, precision=HIGHEST)
    remnant = jnp.exp(running[..., -1:] - running)
    memory = jnp.exp(running[..., -1])[..., None, None] * memory
    memory = memory + jnp.einsum(
        "nhjd,nhje->nhde", keys_all * remnant[..., None], update, precision=HIGHEST
    )
    return (memory, result)


def local(
    moe_input,
    moe_gain,
    routes,
    route_gates,
    expert_gate,
    expert_up,
    expert_down,
    shared_gate,
    shared_up,
    shared_down,
    shared_switch,
    mixed_qkv,
    out_gate,
    beta_logit,
    step_logit,
    conv_weight,
    decay_log,
    decay_bias,
    head_gain,
    lengths,
):
    normed = normalize_rows(moe_input, moe_gain).astype(jnp.bfloat16)
    tok_rows, top_count = routes.shape
    features = normed.shape[1]
    expert_count = lax.axis_size("expert")
    dp_count = lax.axis_size("dp")
    local_experts = expert_gate.shape[0]
    send_count = expert_count * dp_count
    all_experts = send_count * local_experts
    capacity = max(2, min(tok_rows, 5 * tok_rows * top_count // (4 * all_experts)))
    flat_routes = routes.reshape(-1)
    route_count = flat_routes.shape[0]
    one_hot = (flat_routes[:, None] == jnp.arange(all_experts, dtype=jnp.int32)[None, :]).astype(
        jnp.int32
    )
    earlier = jnp.cumsum(one_hot, axis=0) - one_hot
    rank_in = jnp.sum(earlier * one_hot, axis=1)
    slot_index = flat_routes * capacity + rank_in
    slot_tokens = (
        jnp.full((all_experts * capacity,), tok_rows, jnp.int32)
        .at[slot_index]
        .set(jnp.arange(route_count, dtype=jnp.int32) // top_count)
    )
    padded_rows = jnp.concatenate([normed, jnp.zeros((1, features), jnp.bfloat16)], axis=0)
    outgoing = padded_rows[slot_tokens]
    full_gate, full_up, full_down, whole_sgate, whole_sup, whole_sdown = (
        lax.all_gather(expert_gate, "fsdp", axis=2, tiled=True),
        lax.all_gather(expert_up, "fsdp", axis=2, tiled=True),
        lax.all_gather(expert_down, "fsdp", axis=1, tiled=True),
        lax.all_gather(shared_gate, "fsdp", axis=1, tiled=True),
        lax.all_gather(shared_up, "fsdp", axis=1, tiled=True),
        lax.all_gather(shared_down, "fsdp", axis=0, tiled=True),
    )
    shared_result = expert_rows(normed, whole_sgate, whole_sup, whole_sdown)
    switch = jax.nn.sigmoid(jnp.dot(normed.astype(jnp.float32), shared_switch, precision=HIGHEST))
    arrived = lax.all_to_all(
        outgoing.reshape(send_count, local_experts, capacity, features),
        ("expert", "dp"),
        split_axis=0,
        concat_axis=0,
        tiled=True,
    )
    gate_part = jnp.einsum("skcd,kdh->skch", arrived, full_gate, preferred_element_type=jnp.float32)
    up_part = jnp.einsum("skcd,kdh->skch", arrived, full_up, preferred_element_type=jnp.float32)
    hidden = (jax.nn.silu(gate_part) * up_part).astype(jnp.bfloat16)
    produced = jnp.einsum(
        "skch,khd->skcd", hidden, full_down, preferred_element_type=jnp.float32
    ).astype(jnp.bfloat16)
    returned = lax.all_to_all(produced, ("expert", "dp"), split_axis=0, concat_axis=0, tiled=True)
    returned = returned.reshape(all_experts * capacity, features)
    picked_rows = returned[slot_index].astype(jnp.float32).reshape(tok_rows, top_count, features)
    routed_sum = jnp.sum(route_gates[:, :, None] * picked_rows, axis=1)
    moe_output = (routed_sum + switch[:, None] * shared_result).astype(jnp.bfloat16)
    queries, keys_all, values, beta_gate, decays = prepare_heads(
        mixed_qkv, beta_logit, step_logit, conv_weight, decay_log, decay_bias, head_gain
    )
    batch_count, length, heads_count, head_size = queries.shape
    block_size = min(64, length)
    blocks = length // block_size

    def arrange(tensor_in):
        return tensor_in.reshape(batch_count, blocks, block_size, heads_count, head_size).transpose(
            1, 0, 3, 2, 4
        )

    def arrange_small(tensor_in):
        return tensor_in.reshape(batch_count, blocks, block_size, heads_count).transpose(1, 0, 3, 2)

    zero_state = jnp.zeros((batch_count, heads_count, head_size, head_size), jnp.float32)
    final_memory, attended = lax.scan(
        block_rule,
        zero_state,
        (
            arrange(queries),
            arrange(keys_all),
            arrange(values),
            arrange_small(beta_gate),
            arrange_small(decays),
        ),
    )
    attended = attended.transpose(1, 0, 3, 2, 4).reshape(
        batch_count, length, heads_count, head_size
    )
    core_output = gated_output(attended, out_gate, head_gain, lengths)
    return (moe_output, core_output)


def solution(mesh):
    return jax.shard_map(
        local,
        mesh=mesh,
        in_specs=(
            P(("groups", "expert", "fsdp", "dp"), None),
            P(),
            P(("groups", "expert", "fsdp", "dp"), None),
            P(("groups", "expert", "fsdp", "dp"), None),
            P(("expert", "dp"), None, "fsdp"),
            P(("expert", "dp"), None, "fsdp"),
            P(("expert", "dp"), "fsdp", None),
            P(None, "fsdp"),
            P(None, "fsdp"),
            P("fsdp", None),
            P(),
            P(("groups", "expert", "fsdp", "dp"), None, None),
            P(("groups", "expert", "fsdp", "dp"), None, None),
            P(("groups", "expert", "fsdp", "dp"), None, None),
            P(("groups", "expert", "fsdp", "dp"), None, None),
            P(),
            P(),
            P(),
            P(),
            P(("groups", "expert", "fsdp", "dp")),
        ),
        out_specs=(
            P(("groups", "expert", "fsdp", "dp"), None),
            P(("groups", "expert", "fsdp", "dp"), None, None),
        ),
        check_vma=False,
    )
```

profile of v0, /device:TPU:0, one launch (start us, length us, event | category | flops | bytes accessed | tf_op | source)
XLA Modules:
  0.0 389.2 jit_solution(6551267135208959549)
XLA Ops:
  10.9 9.1 %reduce-window.6 = s32[32,10,128]{2,1,0:T(8,128)S(1)} reduce-window(s32[32,10,128]{2,1,0:T(8,128)S(1)} %fusion.87, s32[]{:T(128)} %constant.82.clone.1), window={size=1x1x128 pad=0_0x0_0x127_0}, to_apply=%region_1.0 | reduce-window | flops 5201920 | bytes 327684 | tf_op jit(solution)/shard_map/reduce-window
  20.7 5.2 %scatter_custom_fusion = s32[1600]{0:T(1024)S(1)} fusion(s32[1280]{0:T(1024)S(1)} %fusion.96, s32[1280]{0:T(1024)S(1)} %add_select_fusion, s32[]{:T(128)} %constant.80.clone.1), kind=kCustom, calls=%fused_computation.151 | custom fusion | bytes 6404 | tf_op jit(solution)/shard_map/scatter | solution.py:144
  26.1 6.4 %gather_fusion = bf16[1600,1024]{1,0:T(8,128)(2,1)} fusion(bf16[129,1024]{1,0:T(8,128)(2,1)S(1)} %concatenate.3, s32[2048]{0:T(1024)S(1)} %pad_clamp_fusion.1), kind=kCustom, calls=%fused_computation | custom fusion | bytes 6560000 | tf_op jit(solution)/shard_map/gather | solution.py:147
  32.6 4.6 %reshape.418 = bf16[16,2,50,1024]{3,2,1,0:T(8,128)(2,1)} reshape(bf16[1600,1024]{1,0:T(8,128)(2,1)} %gather_fusion) | data formatting | bytes 6553600 | tf_op jit(solution)/shard_map/reshape | solution.py:159
  37.2 7.1 %copy.95 = bf16[16,2,50,1024]{3,1,2,0:T(2,128)(2,1)} copy(bf16[16,2,50,1024]{3,2,1,0:T(8,128)(2,1)} %reshape.418) | data formatting | bytes 6553600 | tf_op jit(solution)/shard_map/reshape | solution.py:159
  44.3 7.6 %all-to-all-start = ((bf16[16,2,50,1024]{3,1,2,0:T(2,128)(2,1)}), bf16[16,2,50,1024]{3,1,2,0:T(2,128)(2,1)}, u32[]{:S(2)}, u32[]{:S(2)}) async-start(bf16[16,2,50,1024]{3,1,2,0:T(2,128)(2,1)} %copy.95), calls=%async_computation | async-start | bytes 6553600 | tf_op jit(solution)/shard_map/all_to_all | solution.py:158
  61.5 52.1 %all-to-all-done = bf16[16,2,50,1024]{3,1,2,0:T(2,128)(2,1)} async-done(((bf16[16,2,50,1024]{3,1,2,0:T(2,128)(2,1)}), bf16[16,2,50,1024]{3,1,2,0:T(2,128)(2,1)}, u32[]{:S(2)}, u32[]{:S(2)}) %all-to-all-start) | async-done | bytes 3276832 | tf_op jit(solution)/shard_map/all_to_all | solution.py:158
  113.6 6.4 %fusion.47 = f32[2,16,50,512]{3,2,1,0:T(8,128)} fusion(bf16[16,2,50,1024]{3,1,2,0:T(2,128)(2,1)} %all-to-all-done, bf16[2,1024,512]{2,1,0:T(8,128)(2,1)} %all-gather.9.cloned.1.call-done), kind=kOutput, calls=%fused_computation.74 | convolution fusion | flops 1677721600 | bytes 8650752 | tf_op jit(solution)/shard_map/skcd,kdh->skch/dot_general | solution.py:166
  120.1 11.0 %convert_bitcast_fusion = bf16[16,2,50,1024]{3,2,0,1:T(8,128)(2,1)} fusion(bf16[2,512,1024]{2,1,0:T(8,128)(2,1)} %all-gather.11.cloned.1.call-done, f32[2,16,50,512]{3,2,1,0:T(8,128)} %fusion.47, bf16[16,2,50,1024]{3,1,2,0:T(2,128)(2,1)} %all-to-all-done, bf16[2,1024,512]{2,1,0:T(8,128)(2,1)} %all-gather.7.cloned.1.call-done), kind=kOutput, calls=%fused_computation.73 | convolution fusion | flops 3361996800 | bytes 14024704 | tf_op jit(solution)/shard_map/skch,khd->skcd/dot_general | solution.py:168
  131.0 7.3 %copy.98 = bf16[16,2,50,1024]{3,1,2,0:T(2,128)(2,1)} copy(bf16[16,2,50,1024]{3,2,0,1:T(8,128)(2,1)} %convert_bitcast_fusion) | data formatting | bytes 6553600 | tf_op jit(solution)/shard_map/convert_element_type | solution.py:170
  138.3 15.7 %all-to-all-start.1 = ((bf16[16,2,50,1024]{3,1,2,0:T(2,128)(2,1)}), bf16[16,2,50,1024]{3,1,2,0:T(2,128)(2,1)}, u32[]{:S(2)}, u32[]{:S(2)}) async-start(bf16[16,2,50,1024]{3,1,2,0:T(2,128)(2,1)} %copy.98), calls=%async_computation.1 | async-start | bytes 6553600 | tf_op jit(solution)/shard_map/all_to_all | solution.py:171
  155.2 189.7 %while.13 = (s32[]{:T(128)}, f32[1,16,128,128]{3,2,1,0:T(8,128)S(1)}, f32[2,1,16,64,128]{4,3,2,1,0:T(8,128)}, f32[2,1,16,64]{3,0,2,1:T(2,128)S(1)}, f32[2,1,16,6...) while((s32[]{:T(128)}, ...), condition=%wide.region_10.11_spmd.clone, body=%wide.region_8.10_spmd.clone.sunk | while | flops 1009672256 | bytes 27050084 | solution.py:192
  155.6 2.0 convolution_multiply_fusion.7
  157.6 1.9 constant_dynamic-slice_fusion.5
  159.7 2.2 fusion.146
  163.8 80.0 %custom-call.12 = f32[16,1,64,64]{2,3,1,0:T(8,128)} custom-call(f32[16,1,64,64]{3,2,1,0:T(8,128)} %fusion.148), custom_call_target="InvertDiagBlocksLowerTriangular" | custom-call | tf_op jit(solution)/shard_map/while/body/eval_jaxpr/jit(_solve_triangular)/vmap()/triangular_solve | solution.py:90
  243.8 2.2 fusion.149
  247.8 2.1 fusion.150
  250.3 2.0 convolution_multiply_fusion.7
  254.5 2.2 fusion.146
  258.6 80.0 %custom-call.12 = f32[16,1,64,64]{2,3,1,0:T(8,128)} custom-call(f32[16,1,64,64]{3,2,1,0:T(8,128)} %fusion.148), custom_call_target="InvertDiagBlocksLowerTriangular" | custom-call | tf_op jit(solution)/shard_map/while/body/eval_jaxpr/jit(_solve_triangular)/vmap()/triangular_solve | solution.py:90
  338.6 2.2 fusion.149
  342.6 2.1 fusion.150
  344.9 1.9 copy.109
  348.7 2.2 fusion.77
  352.0 2.3 fusion.103
  354.3 4.9 %copy.99 = bf16[16,2,50,1024]{3,2,1,0:T(8,128)(2,1)} copy(bf16[16,2,50,1024]{3,1,2,0:T(2,128)(2,1)} %all-to-all-done.1) | data formatting | bytes 6553600 | tf_op jit(solution)/shard_map/all_to_all | solution.py:171
  359.2 3.2 reshape.419
  362.3 5.1 %gather_fusion.1 = bf16[1280,1024]{1,0:T(8,128)(2,1)} fusion(bf16[1600,1024]{1,0:T(8,128)(2,1)S(1)} %reshape.419, s32[2048]{0:T(1024)S(1)} %pad_clamp_fusion), kind=kCustom, calls=%fused_computation.1 | custom fusion | bytes 5248000 | tf_op jit(solution)/shard_map/gather | solution.py:173
  367.4 6.3 %reshape.425 = f32[128,10,1024]{2,1,0:T(8,128)} reshape(bf16[1280,1024]{1,0:T(8,128)(2,1)} %gather_fusion.1) | data formatting | bytes 7864320 | tf_op jit(solution)/shard_map/convert_element_type | solution.py:173
  373.8 5.2 %multiply_reduce_fusion = f32[128,1024]{1,0:T(8,128)S(1)} fusion(f32[128,10,1024]{2,1,0:T(8,128)} %reshape.425, f32[128,10]{1,0:T(8,128)S(1)} %copy-done.10), kind=kLoop, calls=%fused_computation.65 | loop fusion | flops 2490368 | bytes 5772288 | tf_op jit(solution)/shard_map/reduce_sum | solution.py:174
  379.1 2.8 fusion.66
  (161 shorter events, 27.3 us)
Async XLA Ops:
  7.2 344.5 %copy-start = (f32[1024]{0:T(1024)S(1)}, f32[1024]{0:T(1024)}, u32[]{:S(2)}) copy-start(f32[1024]{0:T(1024)} %param.32) | copy-start | bytes 12292
  7.2 2.8 copy-start.15
  7.2 3.2 copy-start.9
  7.2 54.3 %all-gather.9.cloned.1.call-start = ((), (), s32[]{:S(2)}) async-start(), calls=%async_computation.3 | async-start | bytes 3145728 | tf_op jit(solution)/shard_map/all_gather | solution.py:150
  7.9 112.1 %all-gather.11.cloned.1.call-start = ((), (), s32[]{:S(2)}) async-start(), calls=%async_computation.4 | async-start | bytes 3145728 | tf_op jit(solution)/shard_map/all_gather | solution.py:151
  8.7 17.2 %copy-start.21 = (f32[1024]{0:T(1024)S(1)}, f32[1024]{0:T(1024)}, u32[]{:S(2)}) copy-start(f32[1024]{0:T(1024)} %param.23) | copy-start | bytes 12292
  8.7 111.4 %all-gather.7.cloned.1.call-start = ((), (), s32[]{:S(2)}) async-start(), calls=%async_computation.2 | async-start | bytes 3145728 | tf_op jit(solution)/shard_map/all_gather | solution.py:149
  9.4 342.6 %all-gather.13.cloned.1.call-start = ((), (), s32[]{:S(2)}) async-start(), calls=%async_computation.5 | async-start | bytes 1572864 | tf_op jit(solution)/shard_map/all_gather | solution.py:152
  20.6 5.4 %copy-start.16 = (s32[1280]{0:T(1024)}, s32[1280]{0:T(1024)S(1)}, u32[]{:S(2)}) copy-start(s32[1280]{0:T(1024)S(1)} %fusion.96) | copy-start | bytes 15364
  44.3 8.8 %copy-start.24 = (f32[16]{0:T(128)S(1)}, f32[16]{0:T(128)}, u32[]{:S(2)}) copy-start(f32[16]{0:T(128)} %param.38) | copy-start | bytes 196
  44.3 8.8 %copy-start.19 = (f32[1,128,16]{1,2,0:T(8,128)S(1)}, f32[1,128,16]{1,2,0:T(8,128)}, u32[]{:S(2)}) copy-start(f32[1,128,16]{1,2,0:T(8,128)} %param.36) | copy-start | bytes 24580
  44.3 8.8 %copy-start.22 = (f32[16]{0:T(128)S(1)}, f32[16]{0:T(128)}, u32[]{:S(2)}) copy-start(f32[16]{0:T(128)} %param.39) | copy-start | bytes 196
  44.3 9.0 %copy-start.8 = (bf16[1,128,4096]{2,1,0:T(8,128)(2,1)S(1)}, bf16[1,128,4096]{2,1,0:T(8,128)(2,1)}, u32[]{:S(2)}) copy-start(bf16[1,128,4096]{2,1,0:T(8,128)(2,1)} %param.33) | copy-start | bytes 3145732
  44.3 69.3 %all-to-all-start = ((bf16[16,2,50,1024]{3,1,2,0:T(2,128)(2,1)}), bf16[16,2,50,1024]{3,1,2,0:T(2,128)(2,1)}, u32[]{:S(2)}, u32[]{:S(2)}) async-start(bf16[16,2,50,1024]{3,1,2,0:T(2,128)(2,1)} %copy.95), calls=%async_computation | async-start | bytes 6553600 | tf_op jit(solution)/shard_map/all_to_all | solution.py:158
  51.9 327.1 %all-gather.17.cloned.1.call-start = ((), (), s32[]{:S(2)}) async-start(), calls=%async_computation.7 | async-start | bytes 1572864 | tf_op jit(solution)/shard_map/all_gather | solution.py:154
  52.5 326.5 %all-gather.15.cloned.1.call-start = ((), (), s32[]{:S(2)}) async-start(), calls=%async_computation.6 | async-start | bytes 1572864 | tf_op jit(solution)/shard_map/all_gather | solution.py:153
  54.9 4.3 %copy-start.20 = (f32[1,128,16]{1,2,0:T(8,128)S(1)}, f32[1,128,16]{1,2,0:T(8,128)}, u32[]{:S(2)}) copy-start(f32[1,128,16]{1,2,0:T(8,128)} %param.35) | copy-start | bytes 24580
  138.3 216.0 %all-to-all-start.1 = ((bf16[16,2,50,1024]{3,1,2,0:T(2,128)(2,1)}), bf16[16,2,50,1024]{3,1,2,0:T(2,128)(2,1)}, u32[]{:S(2)}, u32[]{:S(2)}) async-start(bf16[16,2,50,1024]{3,1,2,0:T(2,128)(2,1)} %copy.98), calls=%async_computation.1 | async-start | bytes 6553600 | tf_op jit(solution)/shard_map/all_to_all | solution.py:171
  155.2 4.5 %copy-start.12 = (f32[2,1,16,64]{3,0,2,1:T(2,128)}, f32[2,1,16,64]{3,0,2,1:T(2,128)S(1)}, u32[]{:S(2)}) copy-start(f32[2,1,16,64]{3,0,2,1:T(2,128)S(1)} %get-tuple-element.228) | copy-start | bytes 24580 | tf_op jit(solution)/shard_map/while
  243.8 2.9 copy-start.1
  243.8 2.9 copy-start.2
  246.7 3.2 copy-start.13
  247.8 2.1 copy-start.3
  249.9 4.5 %copy-start.12 = (f32[2,1,16,64]{3,0,2,1:T(2,128)}, f32[2,1,16,64]{3,0,2,1:T(2,128)S(1)}, u32[]{:S(2)}) copy-start(f32[2,1,16,64]{3,0,2,1:T(2,128)S(1)} %get-tuple-element.228) | copy-start | bytes 24580 | tf_op jit(solution)/shard_map/while
  338.6 2.9 copy-start.1
  338.6 2.9 copy-start.2
  341.5 3.2 copy-start.13
  342.5 2.1 copy-start.3
  347.8 3.1 copy-start.18
  347.9 3.8 copy-start.17
  367.4 6.3 %copy-start.10 = (f32[128,10]{1,0:T(8,128)S(1)}, f32[128,10]{1,0:T(8,128)}, u32[]{:S(2)}) copy-start(f32[128,10]{1,0:T(8,128)} %copy.89) | copy-start | bytes 15364
  373.7 5.3 %copy-start.11 = (f32[128,512]{1,0:T(8,128)S(1)}, f32[128,512]{1,0:T(8,128)}, u32[]{:S(2)}) copy-start(f32[128,512]{1,0:T(8,128)} %fusion.103) | copy-start | bytes 786436
  (6 other events, 9.7 us)
Sparse Core Ops, SparseCore 0:
  9.6 35.7 all-gather.8
  47.0 33.0 all-gather.10
  81.6 33.0 all-gather.6
  116.1 21.2 all-gather.12
  138.8 21.2 all-gather.16
  161.6 21.4 all-gather.14
where the time goes:
time: 396 us; the launch traced here: 389 us
  other arithmetic  183 us (46%)
  local copies, waits for them, and re-layouts  63.6 us (16%)
  waiting for transfers between devices  55.6 us (14%)
  matrix products  47 us (12%)
  starting transfers between devices  23.7 us (6%)
  between operations  15.7 us (4%)
    another operation x4, other arithmetic, block_rule(): jax.scipy.linalg.solve_triangular(system, target, lower=True, unit_diagon...  160 us
    all_to_all x1, waiting for transfers between devices, local(): lax.all_to_all(outgoing.reshape(send_count, local_experts, capacity, feat...  52.1 us
    all_to_all x1, starting transfers between devices, local(): lax.all_to_all(produced, ('expert', 'dp'), split_axis=0, concat_axis=0, t...  15.7 us
    reshape x2, local copies, waits for them, and re-layouts, local(): outgoing.reshape(send_count, local_experts, capacity, features)  11.7 us
    dot_general x1, matrix products, local(): jnp.einsum('skch,khd->skcd', hidden, full_down, preferred_element_type=jn...  11 us
    another operation x3, other arithmetic  9.24 us
  transfers between devices with their start and end apart: 8, of which 1 were waited for; matrix products, arithmetic and copies ran while one was open for 75% of the time, Pallas kernels for 0%

commit v1 on v0

v1 whole, which is shorter than its diff:
```python
import functools
import math

import jax
import jax.numpy as jnp
from jax import lax
from jax.experimental import pallas as pl
from jax.experimental.pallas import tpu as pltpu
from jax.sharding import PartitionSpec as P

EPS = 1e-06
HIGHEST = lax.Precision.HIGHEST


def normalize_rows(rows, gain):
    widened = rows.astype(jnp.float32)
    factor = lax.rsqrt(jnp.mean(widened * widened, axis=-1, keepdims=True) + EPS)
    return widened * factor * gain


def expert_rows(rows, w_gate, w_up, w_down):
    gate_part = jnp.dot(rows, w_gate, preferred_element_type=jnp.float32)
    up_part = jnp.dot(rows, w_up, preferred_element_type=jnp.float32)
    hidden = (jax.nn.silu(gate_part) * up_part).astype(jnp.bfloat16)
    return jnp.dot(hidden, w_down, preferred_element_type=jnp.float32)


def split_bf16(value):
    high = value.astype(jnp.bfloat16)
    low = (value - high.astype(jnp.float32)).astype(jnp.bfloat16)
    return high, low


def product(left, right):
    width = right.shape[1]
    lefts = jnp.concatenate(split_bf16(left), axis=1)
    rights = jnp.concatenate(split_bf16(right), axis=1)
    rights = jnp.concatenate([rights, rights], axis=0)
    both = jnp.dot(lefts, rights, preferred_element_type=jnp.float32)
    return both[:, :width] + both[:, width:]


def product_nt(left, right):
    width = right.shape[0]
    lefts = jnp.concatenate(split_bf16(left), axis=1)
    rights = jnp.concatenate(split_bf16(right), axis=0)
    rights = jnp.concatenate([rights, rights], axis=1)
    both = lax.dot_general(
        lefts, rights, (((1,), (1,)), ((), ())), preferred_element_type=jnp.float32
    )
    return both[:, :width] + both[:, width:]


def sigmoid(value):
    return 1.0 / (1.0 + jnp.exp(-value))


def conv_rows(rows, taps):
    widened = rows.astype(jnp.float32)
    count = taps.shape[0]
    position = lax.broadcasted_iota(jnp.int32, widened.shape, 0)
    total = taps[count - 1 : count, :] * widened
    for back in range(1, count):
        moved = jnp.where(position >= back, pltpu.roll(widened, back, 0), 0.0)
        total = total + taps[count - 1 - back : count - back, :] * moved
    return total * sigmoid(total)


def unit_rows(rows):
    return rows * lax.rsqrt(jnp.sum(rows * rows, axis=-1, keepdims=True) + EPS)


def mixer_prepare(beta_ref, step_ref, log_ref, bias_ref, run_t_ref, run_ref, gate_ref):
    length, heads = step_ref.shape
    row = lax.broadcasted_iota(jnp.int32, (length, length), 0)
    col = lax.broadcasted_iota(jnp.int32, (length, length), 1)
    step = step_ref[...] + bias_ref[...]
    softplus = jnp.maximum(step, 0.0) + jnp.log1p(jnp.exp(-jnp.abs(step)))
    decay = -jnp.exp(log_ref[...]) * softplus
    lower = jnp.where(row >= col, 1.0, 0.0).astype(jnp.bfloat16)
    high, low = split_bf16(decay)
    rest = (decay - high.astype(jnp.float32) - low.astype(jnp.float32)).astype(jnp.bfloat16)
    running = jnp.zeros((length, heads), jnp.float32)
    for piece in (rest, low, high):
        running = running + jnp.dot(lower, piece, preferred_element_type=jnp.float32)
    padded = jnp.concatenate(
        [running, jnp.zeros((length, length - heads), jnp.float32)], axis=1
    )
    run_ref[...] = padded
    run_t_ref[...] = jnp.transpose(padded)
    gate_ref[...] = jnp.concatenate(
        [sigmoid(beta_ref[...]), jnp.zeros((length, length - heads), jnp.float32)], axis=1
    )


def mixer_group(
    group, key_heads, total_heads, repeat, size,
    qkv_ref, gate_in_ref, taps_ref, gain_ref, live, run_t_ref, run_ref, gate_ref, out_ref,
):
    length = qkv_ref.shape[0]
    span = key_heads * size
    wide = span * repeat

    def columns(base, width):
        return pl.ds(pl.multiple_of(base + group * width, size), width)

    row = lax.broadcasted_iota(jnp.int32, (length, length), 0)
    col = lax.broadcasted_iota(jnp.int32, (length, length), 1)
    q_cols = columns(0, span)
    k_cols = columns(total_heads * size, span)
    v_cols = columns(2 * total_heads * size, wide)
    queries = conv_rows(qkv_ref[:, q_cols], taps_ref[:, q_cols])
    keys = conv_rows(qkv_ref[:, k_cols], taps_ref[:, k_cols])
    values = conv_rows(qkv_ref[:, v_cols], taps_ref[:, v_cols])
    running_all, gates_all = run_ref[...], gate_ref[...]
    systems, scores, targets = [], [], []
    for key_head in range(key_heads):
        here = slice(key_head * size, (key_head + 1) * size)
        query = unit_rows(queries[:, here]) * (1.0 / math.sqrt(size))
        key = unit_rows(keys[:, here])
        both = product_nt(jnp.concatenate([query, key], axis=0), key)
        for part in range(repeat):
            local_head = key_head * repeat + part
            head = group * (key_heads * repeat) + local_head
            run_col = jnp.sum(jnp.where(col == head, running_all, 0.0), axis=1, keepdims=True)
            beta = jnp.sum(jnp.where(col == head, gates_all, 0.0), axis=1, keepdims=True)
            run_row = run_t_ref[pl.ds(head, 1), :]
            spread = jnp.where(row >= col, run_col - run_row, 0.0)
            factors = jnp.where(row >= col, jnp.exp(spread), 0.0)
            scores.append(both[:length] * factors)
            systems.append(jnp.where(row > col, beta * both[length:] * factors, 0.0))
            targets.append(beta * values[:, local_head * size : (local_head + 1) * size])
    eye = jnp.where(row == col, 1.0, 0.0)
    block = 8
    near = (row // block) == (col // block)
    firsts = [jnp.where(near, system, 0.0) for system in systems]
    seconds = [product(first, first) for first in firsts]
    fourths = [product(second, second) for second in seconds]
    inverses = [
        eye - first + second - product(first, second) for first, second in zip(firsts, seconds)
    ]
    inverses = [
        inverse + product(inverse, fourth) for inverse, fourth in zip(inverses, fourths)
    ]
    while block < length:
        joined = ((row // (2 * block)) == (col // (2 * block))) & ((row // block) != (col // block))
        links = [jnp.where(joined, system, 0.0) for system in systems]
        halves = [product(link, inverse) for link, inverse in zip(links, inverses)]
        inverses = [
            inverse - product(inverse, half) for inverse, half in zip(inverses, halves)
        ]
        block = 2 * block
    updates = [product(inverse, target) for inverse, target in zip(inverses, targets)]
    results = [product(score, update) for score, update in zip(scores, updates)]
    position = lax.broadcasted_iota(jnp.int32, (length, size), 0)
    for local_head, attended in enumerate(results):
        head = group * (key_heads * repeat) + local_head
        head_cols = pl.ds(pl.multiple_of(head * size, size), size)
        factor = lax.rsqrt(jnp.mean(attended * attended, axis=-1, keepdims=True) + EPS)
        gate = gate_in_ref[:, head_cols].astype(jnp.float32)
        gated = attended * factor * gain_ref[...] * (gate * sigmoid(gate))
        out_ref[:, head_cols] = jnp.where(position < live, gated, 0.0).astype(jnp.bfloat16)


def mixer_kernel(
    key_heads, total_heads, repeat, size,
    live_ref, qkv_ref, gate_in_ref, beta_ref, step_ref, taps_ref, log_ref, bias_ref, gain_ref,
    out_ref, run_t_ref, run_ref, gate_ref,
):
    request = pl.program_id(0)
    mixer_prepare(beta_ref, step_ref, log_ref, bias_ref, run_t_ref, run_ref, gate_ref)

    @pl.loop(0, total_heads // key_heads)
    def _(group):
        mixer_group(
            group, key_heads, total_heads, repeat, size,
            qkv_ref, gate_in_ref, taps_ref, gain_ref, live_ref[request],
            run_t_ref, run_ref, gate_ref, out_ref,
        )


def mixer(
    mixed_qkv, out_gate, beta_logit, step_logit, conv_weight, decay_log, decay_bias, head_gain, lengths
):
    requests, length, channels = mixed_qkv.shape
    heads = decay_log.shape[0]
    size = head_gain.shape[0]
    total_heads = (channels - heads * size) // (2 * size)
    repeat = heads // total_heads

    def whole(array):
        return pl.BlockSpec(array.shape, lambda r: (0,) * array.ndim)

    def one(array):
        return pl.BlockSpec((None,) + array.shape[1:], lambda r: (r, 0, 0))

    small = [conv_weight, decay_log[None, :], decay_bias[None, :], head_gain[None, :]]
    return pl.pallas_call(
        functools.partial(mixer_kernel, 2, total_heads, repeat, size),
        grid=(requests,),
        out_shape=jax.ShapeDtypeStruct(out_gate.shape, jnp.bfloat16),
        in_specs=[pl.BlockSpec(memory_space=pltpu.SMEM)]
        + [one(array) for array in (mixed_qkv, out_gate, beta_logit, step_logit)]
        + [whole(array) for array in small],
        out_specs=one(out_gate),
        scratch_shapes=[pltpu.VMEM((length, length), jnp.float32)] * 3,
        compiler_params=pltpu.CompilerParams(vmem_limit_bytes=32 * 1024 * 1024),
        cost_estimate=pl.CostEstimate(
            flops=20_000_000_000, bytes_accessed=4_000_000, transcendentals=0
        ),
    )(lengths, mixed_qkv, out_gate, beta_logit, step_logit, *small)


def dense_experts(
    normed, routes, route_gates, expert_gate, expert_up, expert_down,
    shared_gate, shared_up, shared_down, shared_switch,
):
    tokens, features = normed.shape
    ways = ("expert", "fsdp")
    experts = lax.axis_size("expert") * lax.axis_size("dp") * expert_gate.shape[0]
    names = jnp.arange(experts, dtype=jnp.int32)
    share = jnp.sum(
        jnp.where(routes[:, :, None] == names, route_gates[:, :, None], 0.0), axis=1
    )
    high, low = split_bf16(share)
    pad = jnp.zeros((tokens, 128 - 2 * experts), jnp.bfloat16)
    rows = jnp.concatenate([normed, high, low, pad], axis=1)
    rows = lax.all_gather(rows, ways, axis=0, tiled=True)
    gate = lax.all_gather(expert_gate, "dp", axis=0, tiled=True)
    up = lax.all_gather(expert_up, "dp", axis=0, tiled=True)
    down = lax.all_gather(expert_down, "dp", axis=0, tiled=True)
    held = gate.shape[0]
    first = lax.axis_index("expert") * held
    shares = lax.dynamic_slice_in_dim(rows, features + first, held, 1).astype(
        jnp.float32
    ) + lax.dynamic_slice_in_dim(rows, features + experts + first, held, 1).astype(jnp.float32)
    every = rows[:, :features]
    gates = jnp.einsum("td,edh->teh", every, gate, preferred_element_type=jnp.float32)
    ups = jnp.einsum("td,edh->teh", every, up, preferred_element_type=jnp.float32)
    hidden = (jax.nn.silu(gates) * ups * shares[:, :, None]).astype(jnp.bfloat16)
    partial = jnp.einsum("teh,ehd->td", hidden, down, preferred_element_type=jnp.float32)
    near = lax.axis_size("fsdp") * tokens
    start = lax.axis_index("expert") * near
    mine = lax.dynamic_slice_in_dim(every, start, near, 0)
    switch = jax.nn.sigmoid(jnp.dot(mine.astype(jnp.float32), shared_switch, precision=HIGHEST))
    shared = switch[:, None] * expert_rows(mine, shared_gate, shared_up, shared_down)
    partial = lax.dynamic_update_slice_in_dim(
        partial, lax.dynamic_slice_in_dim(partial, start, near, 0) + shared, start, 0
    ).astype(jnp.bfloat16)
    return lax.psum_scatter(partial, ways, scatter_dimension=0, tiled=True)


def local(
    moe_input,
    moe_gain,
    routes,
    route_gates,
    expert_gate,
    expert_up,
    expert_down,
    shared_gate,
    shared_up,
    shared_down,
    shared_switch,
    mixed_qkv,
    out_gate,
    beta_logit,
    step_logit,
    conv_weight,
    decay_log,
    decay_bias,
    head_gain,
    lengths,
):
    core_output = mixer(
        mixed_qkv, out_gate, beta_logit, step_logit, conv_weight, decay_log, decay_bias, head_gain, lengths
    )
    normed = normalize_rows(moe_input, moe_gain).astype(jnp.bfloat16)
    if lax.axis_size("expert") * lax.axis_size("fsdp") * expert_gate.shape[0] <= 64:
        moe_output = dense_experts(
            normed, routes, route_gates, expert_gate, expert_up, expert_down,
            shared_gate, shared_up, shared_down, shared_switch,
        )
        return (moe_output, core_output)
    tok_rows, top_count = routes.shape
    features = normed.shape[1]
    expert_count = lax.axis_size("expert")
    dp_count = lax.axis_size("dp")
    local_experts = expert_gate.shape[0]
    send_count = expert_count * dp_count
    all_experts = send_count * local_experts
    capacity = max(2, min(tok_rows, 5 * tok_rows * top_count // (4 * all_experts)))
    flat_routes = routes.reshape(-1)
    route_count = flat_routes.shape[0]
    one_hot = (flat_routes[:, None] == jnp.arange(all_experts, dtype=jnp.int32)[None, :]).astype(
        jnp.int32
    )
    earlier = jnp.cumsum(one_hot, axis=0) - one_hot
    rank_in = jnp.sum(earlier * one_hot, axis=1)
    slot_index = flat_routes * capacity + rank_in
    slot_tokens = (
        jnp.full((all_experts * capacity,), tok_rows, jnp.int32)
        .at[slot_index]
        .set(jnp.arange(route_count, dtype=jnp.int32) // top_count)
    )
    padded_rows = jnp.concatenate([normed, jnp.zeros((1, features), jnp.bfloat16)], axis=0)
    outgoing = padded_rows[slot_tokens]
    full_gate, full_up, full_down, whole_sgate, whole_sup, whole_sdown = (
        lax.all_gather(expert_gate, "fsdp", axis=2, tiled=True),
        lax.all_gather(expert_up, "fsdp", axis=2, tiled=True),
        lax.all_gather(expert_down, "fsdp", axis=1, tiled=True),
        lax.all_gather(shared_gate, "fsdp", axis=1, tiled=True),
        lax.all_gather(shared_up, "fsdp", axis=1, tiled=True),
        lax.all_gather(shared_down, "fsdp", axis=0, tiled=True),
    )
    shared_result = expert_rows(normed, whole_sgate, whole_sup, whole_sdown)
    switch = jax.nn.sigmoid(jnp.dot(normed.astype(jnp.float32), shared_switch, precision=HIGHEST))
    arrived = lax.all_to_all(
        outgoing.reshape(send_count, local_experts, capacity, features),
        ("expert", "dp"),
        split_axis=0,
        concat_axis=0,
        tiled=True,
    )
    gate_part = jnp.einsum("skcd,kdh->skch", arrived, full_gate, preferred_element_type=jnp.float32)
    up_part = jnp.einsum("skcd,kdh->skch", arrived, full_up, preferred_element_type=jnp.float32)
    hidden = (jax.nn.silu(gate_part) * up_part).astype(jnp.bfloat16)
    produced = jnp.einsum(
        "skch,khd->skcd", hidden, full_down, preferred_element_type=jnp.float32
    ).astype(jnp.bfloat16)
    returned = lax.all_to_all(produced, ("expert", "dp"), split_axis=0, concat_axis=0, tiled=True)
    returned = returned.reshape(all_experts * capacity, features)
    picked_rows = returned[slot_index].astype(jnp.float32).reshape(tok_rows, top_count, features)
    routed_sum = jnp.sum(route_gates[:, :, None] * picked_rows, axis=1)
    moe_output = (routed_sum + switch[:, None] * shared_result).astype(jnp.bfloat16)
    return (moe_output, core_output)


def solution(mesh):
    return jax.shard_map(
        local,
        mesh=mesh,
        in_specs=(
            P(("groups", "expert", "fsdp", "dp"), None),
            P(),
            P(("groups", "expert", "fsdp", "dp"), None),
            P(("groups", "expert", "fsdp", "dp"), None),
            P(("expert", "dp"), None, "fsdp"),
            P(("expert", "dp"), None, "fsdp"),
            P(("expert", "dp"), "fsdp", None),
            P(None, "fsdp"),
            P(None, "fsdp"),
            P("fsdp", None),
            P(),
            P(("groups", "expert", "fsdp", "dp"), None, None),
            P(("groups", "expert", "fsdp", "dp"), None, None),
            P(("groups", "expert", "fsdp", "dp"), None, None),
            P(("groups", "expert", "fsdp", "dp"), None, None),
            P(),
            P(),
            P(),
            P(),
            P(("groups", "expert", "fsdp", "dp")),
        ),
        out_specs=(
            P(("groups", "expert", "fsdp", "dp"), None),
            P(("groups", "expert", "fsdp", "dp"), None, None),
        ),
        check_vma=False,
    )
```

time: 396 us -> 276 us (0.70); the launches traced: 389 us -> 275 us
  other arithmetic: 183 us -> 9.66 us
  waiting for transfers between devices: 55.6 us -> 200 us
  local copies, waits for them, and re-layouts: 63.6 us -> 5.39 us
  starting transfers between devices: 23.7 us -> 0.19 us
  matrix products: 47 us -> 31.2 us
  Pallas kernels: 0 us -> 13.9 us
    another operation x9 -> x0, other arithmetic: 170 us -> none  [the longest x4 160 us: block_rule(): jax.scipy.linalg.solve_triangular(system, target, lower=True, unit_diagon...]
    all_gather x6 -> x4, waiting for transfers between devices: 0.07 us -> 117 us  [the longest x1 96.3 us: dense_experts(): rows = lax.all_gather(rows, ways, axis=0, tiled=True)]
    reduce_scatter x0 -> x1, waiting for transfers between devices: none -> 81 us  [dense_experts(): return lax.psum_scatter(partial, ways, scatter_dimension=0, tiled=True)]
    all_to_all x2 -> x0, waiting for transfers between devices: 52.1 us -> none  [the longest x1 52.1 us: local(): lax.all_to_all(outgoing.reshape(send_count, local_experts, capacity, feat...]
    all_to_all x2 -> x0, starting transfers between devices: 23.3 us -> none  [the longest x1 15.7 us: local(): lax.all_to_all(produced, ('expert', 'dp'), split_axis=0, concat_axis=0, t...]
    reshape x6 -> x0, local copies, waits for them, and re-layouts: 15.2 us -> none  [the longest x2 11.7 us: local(): outgoing.reshape(send_count, local_experts, capacity, features)]
    pallas_call x0 -> x1, Pallas kernels: none -> 13.9 us  [mixer(): pl.pallas_call(functools.partial(mixer_kernel, 2, total_heads, repeat, si...]
    convert_element_type x2 -> x0, local copies, waits for them, and re-layouts: 13.6 us -> none  [the longest x1 7.29 us: local(): produced = jnp.einsum('skch,khd->skcd', hidden, full_down, preferred_elem...]
  transfers between devices with their start and end apart: 8 -> 5, of which waited for: 1 -> 5; matrix products, arithmetic and copies ran while one was open for 75% -> 6% of each run, Pallas kernels for 0% -> 5%
where the time goes in v1:
time: 276 us; the launch traced here: 275 us
  waiting for transfers between devices  200 us (72%)
  matrix products  31.2 us (11%)
  between operations  14.6 us (5%)
  Pallas kernels  13.9 us (5%)
  other arithmetic  9.66 us (4%)
  local copies, waits for them, and re-layouts  5.39 us (2%)
    all_gather x1, waiting for transfers between devices, dense_experts(): rows = lax.all_gather(rows, ways, axis=0, tiled=True)  96.3 us
    reduce_scatter x1, waiting for transfers between devices, dense_experts(): return lax.psum_scatter(partial, ways, scatter_dimension=0, tiled=True)  81 us
    dot_general x1, matrix products, dense_experts(): jnp.einsum('teh,ehd->td', hidden, down, preferred_element_type=jnp.float32)  16.4 us
    pallas_call x1, Pallas kernels, mixer(): pl.pallas_call(functools.partial(mixer_kernel, 2, total_heads, repeat, si...  13.9 us
    all_gather x1, waiting for transfers between devices, dense_experts(): up = lax.all_gather(expert_up, 'dp', axis=0, tiled=True)  13.2 us
    dot_general x1, matrix products, dense_experts(): jnp.einsum('td,edh->teh', every, gate, preferred_element_type=jnp.float32)  11 us
    convert_element_type x1, other arithmetic, dense_experts(): partial = lax.dynamic_update_slice_in_dim(partial, lax.dynamic_slice_in_d...  6.02 us
  transfers between devices with their start and end apart: 5, of which 5 were waited for; matrix products, arithmetic and copies ran while one was open for 6% of the time, Pallas kernels for 5%

profile of v1, /device:TPU:0, one launch (start us, length us, event | category | flops | bytes accessed | tf_op | source)
XLA Modules:
  0.0 275.2 jit_solution(6619161528657535381)
XLA Ops:
  7.2 0.0 all-gather.5.cloned.1.call-start
  7.2 1.2 copy.37
  8.4 0.2 fusion.8
  8.6 0.7 select_reduce_fusion
  9.3 0.9 fusion.10
  10.2 0.1 pad.3.clone
  10.3 0.9 maximum_maximum_fusion
  11.3 0.0 all-gather.7.cloned.1.call-start
  11.3 0.7 all-gather.7.cloned.1.call-update
  12.0 0.0 all-gather.11.cloned.1.call-start
  12.1 0.7 all-gather.11.cloned.1.call-update
  12.7 0.0 all-gather.9.cloned.1.call-start
  12.8 0.5 all-gather.9.cloned.1.call-update
  13.3 0.0 reduce-scatter.2.cloned.1.call-start
  13.4 96.3 %all-gather.5.cloned.1.call-done = bf16[2048,1152]{0,1:T(8,128)(2,1)} async-done(((bf16[128,1152]{0,1:T(8,128)(2,1)}), bf16[2048,1152]{0,1:T(8,128)(2,1)}) %all-gather.5.cloned.1.call-update) | async-done | bytes 4718608 | tf_op jit(solution)/shard_map/all_gather | solution.py:228
  109.7 2.5 slice.4
  112.2 0.3 fusion.15
  112.5 0.9 convert_add_fusion
  113.4 0.8 copy-done.7
  114.2 0.3 fusion.13
  114.5 5.5 %all-gather.7.cloned.1.call-done = bf16[4,1024,256]{2,1,0:T(8,128)(2,1)} async-done(((bf16[2,1024,256]{2,1,0:T(8,128)(2,1)}), bf16[4,1024,256]{2,1,0:T(8,128)(2,1)}) %all-gather.7.cloned.1.call-update) | async-done | bytes 2097168 | tf_op jit(solution)/shard_map/all_gather | solution.py:229
  120.0 11.0 %fusion.1 = f32[2048,4,256]{2,0,1:T(8,128)} fusion(bf16[4,1024,256]{2,1,0:T(8,128)(2,1)} %all-gather.7.cloned.1.call-done, bf16[2048,1152]{0,1:T(8,128)(2,1)} %all-gather.5.cloned.1.call-done), kind=kOutput, calls=%fused_computation.3 | convolution fusion | flops 4294967296 | bytes 14680064 | tf_op jit(solution)/shard_map/td,edh->teh/dot_general | solution.py:238
  131.1 2.3 all-gather.11.cloned.1.call-done
  133.3 13.2 %all-gather.9.cloned.1.call-done = bf16[4,1024,256]{2,1,0:T(8,128)(2,1)} async-done(((bf16[2,1024,256]{2,1,0:T(8,128)(2,1)}), bf16[4,1024,256]{2,1,0:T(8,128)(2,1)}) %all-gather.9.cloned.1.call-update) | async-done | bytes 2097168 | tf_op jit(solution)/shard_map/all_gather | solution.py:230
  146.5 16.4 %convolution_bitcast_fusion = f32[2048,1024]{1,0:T(8,128)} fusion(bf16[4,256,1024]{2,1,0:T(8,128)(2,1)} %all-gather.11.cloned.1.call-done, f32[2048,4,256]{2,0,1:T(8,128)} %fusion.1, bf16[4,1024,256]{2,1,0:T(8,128)(2,1)} %all-gather.9.cloned.1.call-done, f32[2048,4]{0,1:T(4,128)S(1)} %convert_add_fusion, bf16[2048,1152]{0,1:T(8,128)(2,1)} %all-gather.5.cloned.1.call-done), kind=kOutput, calls=%fused_computation.1 | convolution fusion | flops 8604614656 | bytes 25198592 | tf_op jit(solution)/shard_map/teh,ehd->td/dot_general | solution.py:241
  162.9 3.2 %fusion.6 = f32[2048,1024]{1,0:T(8,128)} fusion(f32[2048,1024]{1,0:T(8,128)} %convolution_bitcast_fusion, s32[]{:T(128)S(6)} %select_n.18, bf16[256,1024]{1,0:T(8,128)(2,1)S(1)} %copy-done, bf16[1024,256]{1,0:T(8,128)(2,1)S(1)} %copy-done.12, f32[256]{0:T(256)S(1)} %add_divide_fusion, bf16[2048,1024]{0,1:T(8,128)(2,1)} %copy-done.7, f32[256,256]{1,0:T(8,128)S(1)} %fusion.13), kind=kOutput, calls=%fused_computation.7 | convolution fusion | flops 269352960 | bytes 3934208 | tf_op jit(solution)/shard_map/dot_general | solution.py:25
  166.1 6.0 %convert_element_type.40 = bf16[2048,1024]{1,0:T(8,128)(2,1)} convert(f32[2048,1024]{1,0:T(8,128)} %fusion.6) | non-fusion elementwise | flops 2097152 | bytes 12582912 | tf_op jit(solution)/shard_map/convert_element_type | solution.py:249
  172.2 0.6 copy-done.9
  172.8 0.1 copy.40.beta_ref
  172.9 0.1 copy.41.step_ref
  173.7 13.9 %shard_map.203 = bf16[1,128,2048]{2,1,0:T(8,128)(2,1)} custom-call(s32[1]{0:T(128)S(6)} %copy.47.live_ref, bf16[1,128,4096]{2,1,0:T(8,128)(2,1)S(1)} %copy-done.1, bf16[1,128,2048]{2,1,0:T(8,128)(2,1)S(1)} %copy-done.2, f32[1,128,16]{2,1,0:T(8,128)S(1)} %copy.40.beta_ref, f32[1,128,16]{2,1,0:T(8,128)S(1)} %copy.41.step_ref, f32[4,4096]{1,0:T(4,128)S(1)} %copy-done.3, ...), custom_call_target="tpu_custom_call" | custom-call | flops 20000000000 | bytes 4000000 | tf_op jit(solution)/shard_map/pallas_call | solution.py:198
  187.6 81.0 %reduce-scatter.2.cloned.1.call-done = bf16[128,1024]{1,0:T(8,128)(2,1)} async-done(((bf16[2048,1024]{1,0:T(8,128)(2,1)}), bf16[128,1024]{1,0:T(8,128)(2,1)}) %reduce-scatter.2.cloned.1.call-update) | async-done | bytes 262160 | tf_op jit(solution)/shard_map/reduce_scatter | solution.py:250
  (30 shorter events, 0.1 us)
Async XLA Ops:
  7.2 155.7 %copy-start = (bf16[256,1024]{1,0:T(8,128)(2,1)S(1)}, bf16[256,1024]{1,0:T(8,128)(2,1)}, u32[]{:S(2)}) copy-start(bf16[256,1024]{1,0:T(8,128)(2,1)} %param.29) | copy-start | bytes 1572868
  7.2 102.5 %all-gather.5.cloned.1.call-start = ((), (), s32[]{:S(2)}) async-start(), calls=%async_computation.1 | async-start | bytes 5013504 | tf_op jit(solution)/shard_map/all_gather | solution.py:228
  11.3 108.7 %all-gather.7.cloned.1.call-start = ((), (), s32[]{:S(2)}) async-start(), calls=%async_computation.2 | async-start | bytes 3145728 | tf_op jit(solution)/shard_map/all_gather | solution.py:229
  12.0 121.3 %all-gather.11.cloned.1.call-start = ((), (), s32[]{:S(2)}) async-start(), calls=%async_computation.4 | async-start | bytes 3145728 | tf_op jit(solution)/shard_map/all_gather | solution.py:231
  12.7 133.8 %all-gather.9.cloned.1.call-start = ((), (), s32[]{:S(2)}) async-start(), calls=%async_computation.3 | async-start | bytes 3145728 | tf_op jit(solution)/shard_map/all_gather | solution.py:230
  13.3 255.3 %reduce-scatter.2.cloned.1.call-start = ((), (), s32[]{:S(2)}) async-start(), calls=%async_computation.5 | async-start | bytes 4456448 | tf_op jit(solution)/shard_map/reduce_scatter | solution.py:250
  13.4 98.8 %copy-start.11 = (f32[1024]{0:T(1024)S(1)}, f32[1024]{0:T(1024)}, u32[]{:S(2)}) copy-start(f32[1024]{0:T(1024)} %param.30) | copy-start | bytes 12292
  13.4 100.8 %copy-start.8 = (bf16[1024,256]{1,0:T(8,128)(2,1)S(1)}, bf16[1024,256]{1,0:T(8,128)(2,1)}, u32[]{:S(2)}) copy-start(bf16[1024,256]{1,0:T(8,128)(2,1)} %param.27) | copy-start | bytes 1572868
  112.2 2.0 copy-start.7
  131.0 31.8 %copy-start.12 = (bf16[1024,256]{1,0:T(8,128)(2,1)S(1)}, bf16[1024,256]{1,0:T(8,128)(2,1)}, u32[]{:S(2)}) copy-start(bf16[1024,256]{1,0:T(8,128)(2,1)} %param.28) | copy-start | bytes 1572868
  172.1 0.7 copy-start.9
  172.1 0.8 copy-start.10
  172.1 1.6 copy-start.1
  172.1 1.6 copy-start.2
  172.1 1.6 copy-start.3
  172.1 1.6 copy-start.4
  172.1 1.6 copy-start.5
  172.1 1.6 copy-start.6
Sparse Core Ops, SparseCore 0:
  11.4 98.2 all-gather.4
  111.2 8.7 all-gather.6
  121.5 11.7 all-gather.10
  134.7 11.7 all-gather.8
  172.3 96.3 reduce-scatter.1

commit v2 on v1

--- a/solution.py
+++ b/solution.py
@@ -211,43 +211,279 @@
     )(lengths, mixed_qkv, out_gate, beta_logit, step_logit, *small)
 
 
-def dense_experts(
-    normed, routes, route_gates, expert_gate, expert_up, expert_down,
+MESH = pl.DeviceIdType.MESH
+
+
+def exchange_kernel(
+    top_count,
+    input_ref, gain_ref, routes_ref, weights_ref, gate_ref, up_ref, down_ref,
+    sgate_ref, sup_ref, sdown_ref, switch_ref,
+    out_ref,
+    held, other_gate, other_up, other_down, hidden, shared_hidden, kept, staged,
+    back_far, back_near, back_line,
+    weight_send, weight_recv, line_send, near_send, far_send, held_recv,
+    back_line_send, back_near_send, back_far_send,
+    back_line_recv, back_near_recv, back_far_recv,
+):
+    tokens, features = input_ref.shape
+    groups, expert = lax.axis_index("groups"), lax.axis_index("expert")
+    cross, core = lax.axis_index("fsdp"), lax.axis_index("dp")
+    line, side = expert // 2, expert % 2
+
+    def device(line_at, side_at, cross_at, core_at):
+        return (groups, line_at * 2 + side_at, cross_at, core_at)
+
+    near = device(line, side + (1 - core) * (1 - 2 * side), cross + core * (1 - 2 * cross), core)
+    far = device(line, side + core * (1 - 2 * side), cross + (1 - core) * (1 - 2 * cross), core)
+    sibling = device(line, side, cross, 1 - core)
+    ahead = [device((line + step) % 4, side, cross, core) for step in range(4)]
+    behind = [device((line + 4 - step) % 4, side, cross, core) for step in range(4)]
+
+    lane = lax.broadcasted_iota(jnp.int32, (tokens, 128), 1)
+    per_core = gate_ref.shape[0]
+    experts = 16 * per_core
+    widened = input_ref[...].astype(jnp.float32)
+    factor = lax.rsqrt(jnp.mean(widened * widened, axis=-1, keepdims=True) + EPS)
+    held[0, :, 0:features] = (widened * factor * gain_ref[...]).astype(jnp.bfloat16)
+    share = jnp.zeros((tokens, 128), jnp.float32)
+    for choice in range(top_count):
+        match = (lane % experts) == routes_ref[:, choice : choice + 1]
+        share = share + jnp.where(match, weights_ref[:, choice : choice + 1], 0.0)
+    high = share.astype(jnp.bfloat16).astype(jnp.float32)
+    held[0, :, features : features + 128] = jnp.where(
+        lane < experts, high, share - high
+    ).astype(jnp.bfloat16)
+
+    barrier = pltpu.get_barrier_semaphore()
+    for partner in (near, far, sibling, ahead[1], ahead[2], ahead[3]):
+        pl.semaphore_signal(barrier, inc=1, device_id=partner, device_id_type=MESH)
+    pl.semaphore_wait(barrier, 6)
+
+    def send(source, target, send_sem, recv_sem, partner):
+        copy = pltpu.make_async_remote_copy(
+            src_ref=source, dst_ref=target, send_sem=send_sem, recv_sem=recv_sem,
+            device_id=partner, device_id_type=MESH,
+        )
+        copy.start()
+        return copy
+
+    lines, nears, fars = {}, {}, {}
+
+    def send_near(slot):
+        nears[slot] = send(
+            held.at[slot], held.at[4 + slot], near_send.at[slot], held_recv.at[4 + slot], near
+        )
+
+    def send_far(slot):
+        fars[slot] = send(
+            held.at[slot], held.at[8 + slot], far_send.at[slot], held_recv.at[8 + slot], far
+        )
+
+    def arrived(slot):
+        if slot < 4:
+            lines[slot].wait_recv()
+        elif slot < 8:
+            nears[slot - 4].wait_recv()
+        else:
+            fars[slot - 8].wait_recv()
+
+    for step in (2, 1, 3):
+        lines[step] = send(
+            held.at[0], held.at[step], line_send.at[step], held_recv.at[step], ahead[step]
+        )
+    send_near(0)
+    send_far(0)
+    exchanged = [
+        send(source, target, weight_send.at[at], weight_recv.at[at], sibling)
+        for at, (source, target) in enumerate(
+            [(gate_ref, other_gate), (up_ref, other_up), (down_ref, other_down)]
+        )
+    ]
+
+    def rows_of(slots):
+        return jnp.concatenate([held[slot, :, 0:features] for slot in slots], axis=0)
+
+    def share_of(slots, name):
+        columns = [
+            jnp.sum(
+                jnp.where(
+                    (lane == name) | (lane == name + experts),
+                    held[slot, :, features : features + 128].astype(jnp.float32),
+                    0.0,
+                ),
+                axis=1,
+                keepdims=True,
+            )
+            for slot in slots
+        ]
+        return jnp.concatenate(columns, axis=0)
+
+    def gated(rows, gate, up, scale):
+        gate_part = jnp.dot(rows, gate, preferred_element_type=jnp.float32)
+        up_part = jnp.dot(rows, up, preferred_element_type=jnp.float32)
+        return (gate_part * sigmoid(gate_part) * up_part * scale).astype(jnp.bfloat16)
+
+    width = gate_ref.shape[2]
+    depth = per_core * width
+
+    def experts_on(slots, with_shared):
+        first = expert * (2 * per_core)
+
+        @pl.loop(0, per_core)
+        def _(index):
+            rows = rows_of(slots)
+            at = pl.multiple_of(index * width, width)
+            hidden[:, pl.ds(at, width)] = gated(
+                rows, gate_ref[index], up_ref[index],
+                share_of(slots, first + core * per_core + index),
+            )
+            hidden[:, pl.ds(depth + at, width)] = gated(
+                rows, other_gate[index], other_up[index],
+                share_of(slots, first + (1 - core) * per_core + index),
+            )
+
+        if with_shared:
+            scales = []
+            for slot, live in zip(slots, (1, core, 1 - core, 0)):
+                rows = held[slot, :, 0:features].astype(jnp.float32)
+                total = jnp.sum(rows * switch_ref[...], axis=-1, keepdims=True)
+                scales.append(sigmoid(total) * (jnp.zeros_like(total) + live))
+            shared_hidden[...] = gated(
+                rows_of(slots), sgate_ref[...], sup_ref[...], jnp.concatenate(scales, axis=0)
+            )
+
+        tile = 256
+
+        @pl.loop(0, features // tile)
+        def _(index):
+            columns = pl.ds(pl.multiple_of(index * tile, tile), tile)
+            total = jnp.dot(
+                hidden[:, 0:depth], down_ref[:, columns], preferred_element_type=jnp.float32
+            )
+            total = total + jnp.dot(
+                hidden[:, depth : 2 * depth], other_down[:, columns],
+                preferred_element_type=jnp.float32,
+            )
+            if with_shared:
+                total = total + jnp.dot(
+                    shared_hidden[...], sdown_ref[:, columns], preferred_element_type=jnp.float32
+                )
+            for at, slot in enumerate(slots):
+                part = total[at * tokens : (at + 1) * tokens]
+                if slot < 8:
+                    kept[slot, :, columns] = part
+                else:
+                    staged[slot, :, columns] = part.astype(jnp.bfloat16)
+
+    back_fars, back_nears, back_lines = {}, {}, {}
+
+    def return_far(slot):
+        back_fars[slot] = send(
+            staged.at[8 + slot], back_far.at[slot], back_far_send.at[slot],
+            back_far_recv.at[slot], far,
+        )
+
+    def forward(slot):
+        arrived(slot)
+        send_near(slot)
+        send_far(slot)
+
+    arrived(4)
+    send_far(4)
+    forward(1)
+    forward(3)
+    for copy in exchanged:
+        copy.wait_recv()
+    arrived(8)
+    arrived(12)
+    experts_on((0, 4, 8, 12), True)
+    return_far(0)
+    return_far(4)
+    forward(2)
+    for slot in (5, 7, 6):
+        arrived(slot)
+        send_far(slot)
+    experts_on((1, 3, 5, 7), False)
+    for slot in (9, 11, 13, 15):
+        arrived(slot)
+    experts_on((9, 11, 13, 15), False)
+    for slot in (5, 7, 1, 3):
+        return_far(slot)
+    arrived(10)
+    arrived(14)
+    experts_on((2, 6, 10, 14), False)
+    return_far(6)
+    return_far(2)
+
+    for slot in (4, 5, 7, 6):
+        back_fars[slot].wait_recv()
+        staged[slot] = (kept[slot] + back_far[slot].astype(jnp.float32)).astype(jnp.bfloat16)
+        back_nears[slot - 4] = send(
+            staged.at[slot], back_near.at[slot - 4], back_near_send.at[slot - 4],
+            back_near_recv.at[slot - 4], near,
+        )
+    for slot in (1, 3, 2):
+        back_fars[slot].wait_recv()
+        back_nears[slot].wait_recv()
+        staged[slot] = (
+            kept[slot] + back_far[slot].astype(jnp.float32) + back_near[slot].astype(jnp.float32)
+        ).astype(jnp.bfloat16)
+        back_lines[slot] = send(
+            staged.at[slot], back_line.at[slot], back_line_send.at[slot],
+            back_line_recv.at[slot], behind[slot],
+        )
+    back_fars[0].wait_recv()
+    back_nears[0].wait_recv()
+    total = kept[0] + back_far[0].astype(jnp.float32) + back_near[0].astype(jnp.float32)
+    for slot in (1, 3, 2):
+        back_lines[slot].wait_recv()
+        total = total + back_line[slot].astype(jnp.float32)
+    out_ref[...] = total.astype(jnp.bfloat16)
+    for copies in (lines, nears, fars, back_fars, back_nears, back_lines):
+        for copy in copies.values():
+            copy.wait_send()
+    for copy in exchanged:
+        copy.wait_send()
+
+
+def exchanged_experts(
+    moe_input, moe_gain, routes, route_gates, expert_gate, expert_up, expert_down,
     shared_gate, shared_up, shared_down, shared_switch,
 ):
-    tokens, features = normed.shape
-    ways = ("expert", "fsdp")
-    experts = lax.axis_size("expert") * lax.axis_size("dp") * expert_gate.shape[0]
-    names = jnp.arange(experts, dtype=jnp.int32)
-    share = jnp.sum(
-        jnp.where(routes[:, :, None] == names, route_gates[:, :, None], 0.0), axis=1
-    )
-    high, low = split_bf16(share)
-    pad = jnp.zeros((tokens, 128 - 2 * experts), jnp.bfloat16)
-    rows = jnp.concatenate([normed, high, low, pad], axis=1)
-    rows = lax.all_gather(rows, ways, axis=0, tiled=True)
-    gate = lax.all_gather(expert_gate, "dp", axis=0, tiled=True)
-    up = lax.all_gather(expert_up, "dp", axis=0, tiled=True)
-    down = lax.all_gather(expert_down, "dp", axis=0, tiled=True)
-    held = gate.shape[0]
-    first = lax.axis_index("expert") * held
-    shares = lax.dynamic_slice_in_dim(rows, features + first, held, 1).astype(
-        jnp.float32
-    ) + lax.dynamic_slice_in_dim(rows, features + experts + first, held, 1).astype(jnp.float32)
-    every = rows[:, :features]
-    gates = jnp.einsum("td,edh->teh", every, gate, preferred_element_type=jnp.float32)
-    ups = jnp.einsum("td,edh->teh", every, up, preferred_element_type=jnp.float32)
-    hidden = (jax.nn.silu(gates) * ups * shares[:, :, None]).astype(jnp.bfloat16)
-    partial = jnp.einsum("teh,ehd->td", hidden, down, preferred_element_type=jnp.float32)
-    near = lax.axis_size("fsdp") * tokens
-    start = lax.axis_index("expert") * near
-    mine = lax.dynamic_slice_in_dim(every, start, near, 0)
-    switch = jax.nn.sigmoid(jnp.dot(mine.astype(jnp.float32), shared_switch, precision=HIGHEST))
-    shared = switch[:, None] * expert_rows(mine, shared_gate, shared_up, shared_down)
-    partial = lax.dynamic_update_slice_in_dim(
-        partial, lax.dynamic_slice_in_dim(partial, start, near, 0) + shared, start, 0
-    ).astype(jnp.bfloat16)
-    return lax.psum_scatter(partial, ways, scatter_dimension=0, tiled=True)
+    tokens, features = moe_input.shape
+    per_core, _, width = expert_gate.shape
+    down = expert_down.reshape(per_core * width, features)
+    block = (tokens, features)
+    bf16, f32, dma = jnp.bfloat16, jnp.float32, pltpu.SemaphoreType.DMA
+    return pl.pallas_call(
+        functools.partial(exchange_kernel, routes.shape[1]),
+        out_shape=jax.ShapeDtypeStruct(block, bf16),
+        in_specs=[pl.BlockSpec(memory_space=pltpu.VMEM)] * 11,
+        out_specs=pl.BlockSpec(memory_space=pltpu.VMEM),
+        scratch_shapes=[
+            pltpu.VMEM((16, tokens, features + 128), bf16),
+            pltpu.VMEM(expert_gate.shape, bf16),
+            pltpu.VMEM(expert_up.shape, bf16),
+            pltpu.VMEM(down.shape, bf16),
+            pltpu.VMEM((4 * tokens, 2 * per_core * width), bf16),
+            pltpu.VMEM((4 * tokens, shared_gate.shape[1]), bf16),
+            pltpu.VMEM((8,) + block, f32),
+            pltpu.VMEM((16,) + block, bf16),
+            pltpu.VMEM((8,) + block, bf16),
+            pltpu.VMEM((4,) + block, bf16),
+            pltpu.VMEM((4,) + block, bf16),
+        ]
+        + [dma((count,)) for count in (3, 3, 4, 4, 8, 16, 4, 4, 8, 4, 4, 8)],
+        compiler_params=pltpu.CompilerParams(
+            collective_id=0, has_side_effects=True, vmem_limit_bytes=56 * 1024 * 1024
+        ),
+        cost_estimate=pl.CostEstimate(
+            flops=13_000_000_000, bytes_accessed=6_000_000, transcendentals=0
+        ),
+    )(
+        moe_input, moe_gain[None, :], routes, route_gates, expert_gate, expert_up, down,
+        shared_gate, shared_up, shared_down, shared_switch[None, :],
+    )
 
 
 def local(
@@ -276,9 +512,9 @@
         mixed_qkv, out_gate, beta_logit, step_logit, conv_weight, decay_log, decay_bias, head_gain, lengths
     )
     normed = normalize_rows(moe_input, moe_gain).astype(jnp.bfloat16)
-    if lax.axis_size("expert") * lax.axis_size("fsdp") * expert_gate.shape[0] <= 64:
-        moe_output = dense_experts(
-            normed, routes, route_gates, expert_gate, expert_up, expert_down,
+    if (lax.axis_size("expert"), lax.axis_size("fsdp"), lax.axis_size("dp")) == (8, 2, 2):
+        moe_output = exchanged_experts(
+            moe_input, moe_gain, routes, route_gates, expert_gate, expert_up, expert_down,
             shared_gate, shared_up, shared_down, shared_switch,
         )
         return (moe_output, core_output)

time: 276 us -> 135 us (0.49)
  waiting for transfers between devices: 200 us -> 0 us
  Pallas kernels: 13.9 us -> 130 us
  matrix products: 31.2 us -> 0 us
  between operations: 14.6 us -> 1.41 us
  other arithmetic: 9.66 us -> 0 us
    all_gather x4 -> x0, waiting for transfers between devices: 117 us -> none  [the longest x1 96.3 us: dense_experts(): rows = lax.all_gather(rows, ways, axis=0, tiled=True)]
    pallas_call x0 -> x1, Pallas kernels: none -> 116 us  [exchanged_experts(): pl.pallas_call(functools.partial(exchange_kernel, routes.shape[1]), out_s...]
    reduce_scatter x1 -> x0, waiting for transfers between devices: 81 us -> none  [dense_experts(): return lax.psum_scatter(partial, ways, scatter_dimension=0, tiled=True)]
    dot_general x5 -> x0, matrix products: 31.2 us -> none  [the longest x1 16.4 us: dense_experts(): jnp.einsum('teh,ehd->td', hidden, down, preferred_element_type=jnp.float32)]
    convert_element_type x3 -> x0, other arithmetic: 6.92 us -> none  [the longest x1 6.02 us: dense_experts(): partial = lax.dynamic_update_slice_in_dim(partial, lax.dynamic_slice_in_d...]
  transfers between devices with their start and end apart: 5 -> 0, of which waited for: 5 -> 0; matrix products, arithmetic and copies ran while one was open for 6% -> 0% of each run, Pallas kernels for 5% -> 0%
where the time goes in v2:
time: 135 us; the launch traced here: 134 us
  Pallas kernels  130 us (96%)
  local copies, waits for them, and re-layouts  3.05 us (2%)
  between operations  1.41 us (1%)
    pallas_call x1, Pallas kernels, exchanged_experts(): pl.pallas_call(functools.partial(exchange_kernel, routes.shape[1]), out_s...  116 us
    pallas_call x1, Pallas kernels, mixer(): pl.pallas_call(functools.partial(mixer_kernel, 2, total_heads, repeat, si...  13.9 us
    unnamed x27, local copies, waits for them, and re-layouts  3.05 us

profile of v2, /device:TPU:0, one launch (start us, length us, event | category | flops | bytes accessed | tf_op | source)
XLA Modules:
  0.0 134.3 jit_solution(6950844761440623691)
XLA Ops:
  0.6 0.0 copy-start.7
  1.3 0.0 copy-done.7
  1.3 0.0 copy-start.8
  1.3 0.7 copy.22.routes_ref
  2.1 0.0 copy-done.8
  2.1 0.0 copy-start.9
  2.1 0.7 copy.23.weights_ref
  2.8 0.0 copy-done.9
  2.8 0.0 copy-start.10
  2.8 0.1 copy.24.beta_ref
  2.9 0.6 copy-done.10
  3.5 0.1 copy.25.step_ref
  3.6 0.0 copy-start
  3.6 0.0 copy-start.1
  3.6 0.0 copy-start.2
  3.6 0.0 copy-start.3
  3.7 0.0 copy-start.4
  3.7 0.0 copy-start.5
  3.7 115.9 %shard_map.203 = bf16[128,1024]{1,0:T(8,128)(2,1)} custom-call(bf16[128,1024]{1,0:T(8,128)(2,1)} %input_ref.1, f32[1,1024]{1,0:T(1,128)} %bitcast.10, s32[128,10]{1,0:T(8,128)} %copy.22.routes_ref, f32[128,10]{1,0:T(8,128)} %copy.23.weights_ref, bf16[2,1024,256]{2,1,0:T(8,128)(2,1)} %gate_ref.1, bf16[2,1024,256]{2,1,0:T(8,128)(2,1)} %up_ref.1, ...), custom_call_target="tpu_custom_call" | custom-call | flops 12999999488 | bytes 6000000 | tf_op jit(solution)/shard_map/pallas_call | solution.py:458
  119.6 0.0 copy-done
  119.6 0.0 copy-done.1
  119.6 0.0 copy-done.2
  119.6 0.0 copy-done.3
  119.6 0.0 copy-done.4
  119.6 0.0 copy-done.5
  119.6 0.0 copy-start.6
  119.7 13.9 %shard_map.204 = bf16[1,128,2048]{2,1,0:T(8,128)(2,1)} custom-call(s32[1]{0:T(128)S(6)} %copy.27.live_ref, bf16[1,128,4096]{2,1,0:T(8,128)(2,1)S(1)} %copy-done, bf16[1,128,2048]{2,1,0:T(8,128)(2,1)S(1)} %copy-done.1, f32[1,128,16]{2,1,0:T(8,128)S(1)} %copy.24.beta_ref, f32[1,128,16]{2,1,0:T(8,128)S(1)} %copy.25.step_ref, f32[4,4096]{1,0:T(4,128)S(1)} %copy-done.2, ...), custom_call_target="tpu_custom_call" | custom-call | flops 20000000000 | bytes 4000000 | tf_op jit(solution)/shard_map/pallas_call | solution.py:198
  133.6 0.0 copy-done.6
  133.6 0.7 copy.28
Async XLA Ops:
  0.6 0.7 copy-start.7
  1.3 0.7 copy-start.8
  2.1 0.7 copy-start.9
  2.8 0.7 copy-start.10
  3.6 116.0 %copy-start = (bf16[1,128,4096]{2,1,0:T(8,128)(2,1)S(1)}, bf16[1,128,4096]{2,1,0:T(8,128)(2,1)}, u32[]{:S(2)}) copy-start(bf16[1,128,4096]{2,1,0:T(8,128)(2,1)} %qkv_ref.1) | copy-start | bytes 3145732
  3.6 116.0 %copy-start.1 = (bf16[1,128,2048]{2,1,0:T(8,128)(2,1)S(1)}, bf16[1,128,2048]{2,1,0:T(8,128)(2,1)}, u32[]{:S(2)}) copy-start(bf16[1,128,2048]{2,1,0:T(8,128)(2,1)} %gate_in_ref.1) | copy-start | bytes 1572868
  3.6 116.0 %copy-start.2 = (f32[4,4096]{1,0:T(4,128)S(1)}, f32[4,4096]{1,0:T(4,128)}, u32[]{:S(2)}) copy-start(f32[4,4096]{1,0:T(4,128)} %taps_ref.1) | copy-start | bytes 196612
  3.6 116.0 %copy-start.3 = (f32[16]{0:T(128)S(1)}, f32[16]{0:T(128)}, u32[]{:S(2)}) copy-start(f32[16]{0:T(128)} %param.36) | copy-start | bytes 196
  3.7 116.0 %copy-start.4 = (f32[16]{0:T(128)S(1)}, f32[16]{0:T(128)}, u32[]{:S(2)}) copy-start(f32[16]{0:T(128)} %param.37) | copy-start | bytes 196
  3.7 116.0 %copy-start.5 = (f32[128]{0:T(128)S(1)}, f32[128]{0:T(128)}, u32[]{:S(2)}) copy-start(f32[128]{0:T(128)} %param.38) | copy-start | bytes 1540
  119.6 13.9 %copy-start.6 = (bf16[128,1024]{1,0:T(8,128)(2,1)S(1)}, bf16[128,1024]{1,0:T(8,128)(2,1)}, u32[]{:S(2)}) copy-start(bf16[128,1024]{1,0:T(8,128)(2,1)} %shard_map.203) | copy-start | bytes 786436

commit v3 on v2

--- a/solution.py
+++ b/solution.py
@@ -215,15 +215,17 @@
 
 
 def exchange_kernel(
-    top_count,
+    top_count, mixer_heads,
     input_ref, gain_ref, routes_ref, weights_ref, gate_ref, up_ref, down_ref,
     sgate_ref, sup_ref, sdown_ref, switch_ref,
-    out_ref,
+    live_ref, qkv_ref, gate_in_ref, beta_ref, step_ref, taps_ref, log_ref, bias_ref, head_gain_ref,
+    out_ref, core_ref,
     held, other_gate, other_up, other_down, hidden, shared_hidden, kept, staged,
     back_far, back_near, back_line,
     weight_send, weight_recv, line_send, near_send, far_send, held_recv,
     back_line_send, back_near_send, back_far_send,
     back_line_recv, back_near_recv, back_far_recv,
+    run_t_ref, run_ref, strength_ref,
 ):
     tokens, features = input_ref.shape
     groups, expert = lax.axis_index("groups"), lax.axis_index("expert")
@@ -236,8 +238,8 @@
     near = device(line, side + (1 - core) * (1 - 2 * side), cross + core * (1 - 2 * cross), core)
     far = device(line, side + core * (1 - 2 * side), cross + (1 - core) * (1 - 2 * cross), core)
     sibling = device(line, side, cross, 1 - core)
-    ahead = [device((line + step) % 4, side, cross, core) for step in range(4)]
-    behind = [device((line + 4 - step) % 4, side, cross, core) for step in range(4)]
+    places = (line, line + 1 - 2 * (line % 2), (line + 2) % 4, 3 - line)
+    paired = [device(place, side, cross, core) for place in places]
 
     lane = lax.broadcasted_iota(jnp.int32, (tokens, 128), 1)
     per_core = gate_ref.shape[0]
@@ -255,7 +257,7 @@
     ).astype(jnp.bfloat16)
 
     barrier = pltpu.get_barrier_semaphore()
-    for partner in (near, far, sibling, ahead[1], ahead[2], ahead[3]):
+    for partner in (near, far, sibling, paired[1], paired[2], paired[3]):
         pl.semaphore_signal(barrier, inc=1, device_id=partner, device_id_type=MESH)
     pl.semaphore_wait(barrier, 6)
 
@@ -287,9 +289,9 @@
         else:
             fars[slot - 8].wait_recv()
 
-    for step in (2, 1, 3):
+    for step in (1, 3, 2):
         lines[step] = send(
-            held.at[0], held.at[step], line_send.at[step], held_recv.at[step], ahead[step]
+            held.at[0], held.at[step], line_send.at[step], held_recv.at[step], paired[step]
         )
     send_near(0)
     send_far(0)
@@ -388,41 +390,28 @@
         send_near(slot)
         send_far(slot)
 
-    arrived(4)
-    send_far(4)
-    forward(1)
-    forward(3)
-    for copy in exchanged:
-        copy.wait_recv()
-    arrived(8)
-    arrived(12)
-    experts_on((0, 4, 8, 12), True)
-    return_far(0)
-    return_far(4)
-    forward(2)
-    for slot in (5, 7, 6):
-        arrived(slot)
-        send_far(slot)
-    experts_on((1, 3, 5, 7), False)
-    for slot in (9, 11, 13, 15):
-        arrived(slot)
-    experts_on((9, 11, 13, 15), False)
-    for slot in (5, 7, 1, 3):
+    def gather_near(slot):
+        arrived(4 + slot)
+        send_far(4 + slot)
+
+    def run(slot):
+        arrived(8 + slot)
+        arrived(12 + slot)
+        experts_on((slot, 4 + slot, 8 + slot, 12 + slot), slot == 0)
+        return_far(4 + slot)
         return_far(slot)
-    arrived(10)
-    arrived(14)
-    experts_on((2, 6, 10, 14), False)
-    return_far(6)
-    return_far(2)
-
-    for slot in (4, 5, 7, 6):
-        back_fars[slot].wait_recv()
-        staged[slot] = (kept[slot] + back_far[slot].astype(jnp.float32)).astype(jnp.bfloat16)
-        back_nears[slot - 4] = send(
-            staged.at[slot], back_near.at[slot - 4], back_near_send.at[slot - 4],
-            back_near_recv.at[slot - 4], near,
-        )
-    for slot in (1, 3, 2):
+
+    def reduce_near(slot):
+        back_fars[4 + slot].wait_recv()
+        staged[4 + slot] = (
+            kept[4 + slot] + back_far[4 + slot].astype(jnp.float32)
+        ).astype(jnp.bfloat16)
+        back_nears[slot] = send(
+            staged.at[4 + slot], back_near.at[slot], back_near_send.at[slot],
+            back_near_recv.at[slot], near,
+        )
+
+    def reduce_line(slot):
         back_fars[slot].wait_recv()
         back_nears[slot].wait_recv()
         staged[slot] = (
@@ -430,8 +419,43 @@
         ).astype(jnp.bfloat16)
         back_lines[slot] = send(
             staged.at[slot], back_line.at[slot], back_line_send.at[slot],
-            back_line_recv.at[slot], behind[slot],
-        )
+            back_line_recv.at[slot], paired[slot],
+        )
+
+    def mix(start, stop):
+        @pl.loop(start, stop)
+        def _(group):
+            mixer_group(
+                group, 2, mixer_heads[0], mixer_heads[1], mixer_heads[2],
+                qkv_ref, gate_in_ref, taps_ref, head_gain_ref, live_ref[0],
+                run_t_ref, run_ref, strength_ref, core_ref,
+            )
+
+    mixer_prepare(beta_ref, step_ref, log_ref, bias_ref, run_t_ref, run_ref, strength_ref)
+    gather_near(0)
+    forward(1)
+    mix(0, 1)
+    gather_near(1)
+    for copy in exchanged:
+        copy.wait_recv()
+    run(0)
+    forward(3)
+    mix(1, 2)
+    gather_near(3)
+    run(1)
+    forward(2)
+    reduce_near(0)
+    gather_near(2)
+    mix(2, 3)
+    reduce_near(1)
+    run(3)
+    reduce_line(1)
+    mix(3, mixer_heads[0] // 2)
+    run(2)
+    reduce_near(3)
+    reduce_line(3)
+    reduce_near(2)
+    reduce_line(2)
     back_fars[0].wait_recv()
     back_nears[0].wait_recv()
     total = kept[0] + back_far[0].astype(jnp.float32) + back_near[0].astype(jnp.float32)
@@ -449,17 +473,24 @@
 def exchanged_experts(
     moe_input, moe_gain, routes, route_gates, expert_gate, expert_up, expert_down,
     shared_gate, shared_up, shared_down, shared_switch,
+    mixed_qkv, out_gate, beta_logit, step_logit, conv_weight, decay_log, decay_bias, head_gain, lengths,
 ):
     tokens, features = moe_input.shape
+    _, length, channels = mixed_qkv.shape
+    size = head_gain.shape[0]
+    heads = decay_log.shape[0]
+    key_heads = (channels - heads * size) // (2 * size)
+    mixer_heads = (key_heads, heads // key_heads, size)
+    vmem = pl.BlockSpec(memory_space=pltpu.VMEM)
     per_core, _, width = expert_gate.shape
     down = expert_down.reshape(per_core * width, features)
     block = (tokens, features)
     bf16, f32, dma = jnp.bfloat16, jnp.float32, pltpu.SemaphoreType.DMA
-    return pl.pallas_call(
-        functools.partial(exchange_kernel, routes.shape[1]),
-        out_shape=jax.ShapeDtypeStruct(block, bf16),
-        in_specs=[pl.BlockSpec(memory_space=pltpu.VMEM)] * 11,
-        out_specs=pl.BlockSpec(memory_space=pltpu.VMEM),
+    moe_output, core_output = pl.pallas_call(
+        functools.partial(exchange_kernel, routes.shape[1], mixer_heads),
+        out_shape=[jax.ShapeDtypeStruct(block, bf16), jax.ShapeDtypeStruct(out_gate.shape[1:], bf16)],
+        in_specs=[vmem] * 11 + [pl.BlockSpec(memory_space=pltpu.SMEM)] + [vmem] * 8,
+        out_specs=[vmem, vmem],
         scratch_shapes=[
             pltpu.VMEM((16, tokens, features + 128), bf16),
             pltpu.VMEM(expert_gate.shape, bf16),
@@ -473,7 +504,8 @@
             pltpu.VMEM((4,) + block, bf16),
             pltpu.VMEM((4,) + block, bf16),
         ]
-        + [dma((count,)) for count in (3, 3, 4, 4, 8, 16, 4, 4, 8, 4, 4, 8)],
+        + [dma((count,)) for count in (3, 3, 4, 4, 8, 16, 4, 4, 8, 4, 4, 8)]
+        + [pltpu.VMEM((length, length), f32)] * 3,
         compiler_params=pltpu.CompilerParams(
             collective_id=0, has_side_effects=True, vmem_limit_bytes=56 * 1024 * 1024
         ),
@@ -483,7 +515,10 @@
     )(
         moe_input, moe_gain[None, :], routes, route_gates, expert_gate, expert_up, down,
         shared_gate, shared_up, shared_down, shared_switch[None, :],
-    )
+        lengths, mixed_qkv[0], out_gate[0], beta_logit[0], step_logit[0],
+        conv_weight, decay_log[None, :], decay_bias[None, :], head_gain[None, :],
+    )
+    return moe_output, core_output[None]
 
 
 def local(
@@ -508,16 +543,17 @@
     head_gain,
     lengths,
 ):
+    sizes = (lax.axis_size("expert"), lax.axis_size("fsdp"), lax.axis_size("dp"))
+    if sizes == (8, 2, 2) and mixed_qkv.shape[0] == 1:
+        return exchanged_experts(
+            moe_input, moe_gain, routes, route_gates, expert_gate, expert_up, expert_down,
+            shared_gate, shared_up, shared_down, shared_switch,
+            mixed_qkv, out_gate, beta_logit, step_logit, conv_weight, decay_log, decay_bias, head_gain, lengths,
+        )
     core_output = mixer(
         mixed_qkv, out_gate, beta_logit, step_logit, conv_weight, decay_log, decay_bias, head_gain, lengths
     )
     normed = normalize_rows(moe_input, moe_gain).astype(jnp.bfloat16)
-    if (lax.axis_size("expert"), lax.axis_size("fsdp"), lax.axis_size("dp")) == (8, 2, 2):
-        moe_output = exchanged_experts(
-            moe_input, moe_gain, routes, route_gates, expert_gate, expert_up, expert_down,
-            shared_gate, shared_up, shared_down, shared_switch,
-        )
-        return (moe_output, core_output)
     tok_rows, top_count = routes.shape
     features = normed.shape[1]
     expert_count = lax.axis_size("expert")

time: 135 us -> 110 us (0.81)
  Pallas kernels: 130 us -> 102 us
  local copies, waits for them, and re-layouts: 3.05 us -> 6.16 us
    pallas_call x2 -> x1, Pallas kernels: 130 us -> 102 us  [exchanged_experts(): pl.pallas_call(functools.partial(exchange_kernel, routes.shape[1], mixer_...]
    unnamed x27 -> x16, local copies, waits for them, and re-layouts: 3.05 us -> 6.16 us
where the time goes in v3:
time: 110 us
  Pallas kernels  102 us (93%)
  local copies, waits for them, and re-layouts  6.16 us (6%)
  between operations  1.31 us (1%)
    pallas_call x1, Pallas kernels, exchanged_experts(): pl.pallas_call(functools.partial(exchange_kernel, routes.shape[1], mixer_...  102 us
    unnamed x16, local copies, waits for them, and re-layouts  6.16 us

profile of v3, /device:TPU:0, one launch (start us, length us, event | category | flops | bytes accessed | tf_op | source)
XLA Modules:
  0.0 109.6 jit_solution(13476698034774794230)
XLA Ops:
  1.3 0.0 copy-start.1
  1.3 0.7 copy-done.1
  2.0 0.0 copy-start.2
  2.0 0.7 copy.24.routes_ref
  2.7 0.0 copy-done.2
  2.7 0.0 copy-start.3
  2.7 0.7 copy.25.weights_ref
  3.5 0.0 copy-done.3
  3.5 0.0 copy-start.4
  3.5 0.7 copy.22
  4.2 0.0 copy-done.4
  4.2 0.7 copy.23
  4.9 102.1 %shard_map.203 = (bf16[128,1024]{1,0:T(8,128)(2,1)}, bf16[128,2048]{1,0:T(8,128)(2,1)}) custom-call(bf16[128,1024]{1,0:T(8,128)(2,1)} %input_ref.1, f32[1,1024]{1,0:T(1,128)} %bitcast.17, s32[128,10]{1,0:T(8,128)} %copy.24.routes_ref, f32[128,10]{1,0:T(8,128)} %copy.25.weights_ref, bf16[2,1024,256]{2,1,0:T(8,128)(2,1)} %gate_ref.1, ...), custom_call_target="tpu_custom_call" | custom-call | flops 12999999488 | bytes 6000000 | tf_op jit(solution)/shard_map/pallas_call | solution.py:489
  107.0 0.0 copy-start
  107.1 1.7 %copy.29 = bf16[128,1024]{1,0:T(8,128)(2,1)} copy(bf16[128,1024]{1,0:T(8,128)(2,1)} %get-tuple-element.8) | data formatting | bytes 524288
  108.8 0.0 copy-done
  108.8 0.8 copy.30
Async XLA Ops:
  1.3 0.7 copy-start.1
  2.0 0.7 copy-start.2
  2.7 0.7 copy-start.3
  3.5 0.7 copy-start.4
  107.0 1.7 %copy-start = (bf16[128,2048]{1,0:T(8,128)(2,1)S(1)}, bf16[128,2048]{1,0:T(8,128)(2,1)}, u32[]{:S(2)}) copy-start(bf16[128,2048]{1,0:T(8,128)(2,1)} %get-tuple-element.5) | copy-start | bytes 1572868

commit v4 on v3

--- a/solution.py
+++ b/solution.py
@@ -442,10 +442,10 @@
     forward(3)
     mix(1, 2)
     gather_near(3)
+    forward(2)
     run(1)
-    forward(2)
+    gather_near(2)
     reduce_near(0)
-    gather_near(2)
     mix(2, 3)
     reduce_near(1)
     run(3)

time: 110 us -> 112 us (1.018)
  Pallas kernels: 102 us -> 105 us
    pallas_call x1, Pallas kernels: 102 us -> 105 us  [exchanged_experts(): pl.pallas_call(functools.partial(exchange_kernel, routes.shape[1], mixer_...]
where the time goes in v4:
time: 112 us
  Pallas kernels  105 us (94%)
  local copies, waits for them, and re-layouts  6.16 us (6%)
  between operations  1.31 us (1%)
    pallas_call x1, Pallas kernels, exchanged_experts(): pl.pallas_call(functools.partial(exchange_kernel, routes.shape[1], mixer_...  105 us
    unnamed x16, local copies, waits for them, and re-layouts  6.16 us

profile of v4, /device:TPU:0, one launch (start us, length us, event | category | flops | bytes accessed | tf_op | source)
XLA Modules:
  0.0 112.1 jit_solution(6912080050982916631)
XLA Ops:
  1.3 0.0 copy-start.1
  1.3 0.7 copy-done.1
  2.0 0.0 copy-start.2
  2.0 0.7 copy.24.routes_ref
  2.7 0.0 copy-done.2
  2.7 0.0 copy-start.3
  2.7 0.7 copy.25.weights_ref
  3.5 0.0 copy-done.3
  3.5 0.0 copy-start.4
  3.5 0.7 copy.22
  4.2 0.0 copy-done.4
  4.2 0.7 copy.23
  4.9 104.7 %shard_map.203 = (bf16[128,1024]{1,0:T(8,128)(2,1)}, bf16[128,2048]{1,0:T(8,128)(2,1)}) custom-call(bf16[128,1024]{1,0:T(8,128)(2,1)} %input_ref.1, f32[1,1024]{1,0:T(1,128)} %bitcast.17, s32[128,10]{1,0:T(8,128)} %copy.24.routes_ref, f32[128,10]{1,0:T(8,128)} %copy.25.weights_ref, bf16[2,1024,256]{2,1,0:T(8,128)(2,1)} %gate_ref.1, ...), custom_call_target="tpu_custom_call" | custom-call | flops 12999999488 | bytes 6000000 | tf_op jit(solution)/shard_map/pallas_call | solution.py:489
  109.6 0.0 copy-start
  109.6 1.7 %copy.29 = bf16[128,1024]{1,0:T(8,128)(2,1)} copy(bf16[128,1024]{1,0:T(8,128)(2,1)} %get-tuple-element.8) | data formatting | bytes 524288
  111.3 0.0 copy-done
  111.3 0.8 copy.30
Async XLA Ops:
  1.3 0.7 copy-start.1
  2.0 0.7 copy-start.2
  2.7 0.7 copy-start.3
  3.5 0.7 copy-start.4
  109.6 1.7 %copy-start = (bf16[128,2048]{1,0:T(8,128)(2,1)S(1)}, bf16[128,2048]{1,0:T(8,128)(2,1)}, u32[]{:S(2)}) copy-start(bf16[128,2048]{1,0:T(8,128)(2,1)} %get-tuple-element.5) | copy-start | bytes 1572868
